TPU v7x, 256 devices: a whole 4x4x8 slice. The times are simulated.
256 devices in a mesh: pipe: 8 (over x, core), seq: 8 (over z), tp: 4 (over y).
Axes of the slice: x: 4, y: 4, z: 8, core: 2. Of those that a mesh axis runs over, the one named last changes fastest.
Arguments:
- query_fwd: bfloat16 [8, 4096, 32, 128], P('pipe', ('seq', 'tp')), may hold values from -60 to 60
- key_fwd: bfloat16 [8, 4096, 32, 128], P('pipe', ('seq', 'tp')), may hold values from -6 to 6
- value_fwd: bfloat16 [8, 4096, 32, 128], P('pipe', ('seq', 'tp')), may hold values from -18 to 18
- query_bwd: bfloat16 [8, 4096, 32, 128], P('pipe', ('seq', 'tp')), may hold values from -60 to 60
- key_bwd: bfloat16 [8, 4096, 32, 128], P('pipe', ('seq', 'tp')), may hold values from -6 to 6
- value_bwd: bfloat16 [8, 4096, 32, 128], P('pipe', ('seq', 'tp')), may hold values from -18 to 18
- grad_mix: bfloat16 [8, 4096, 32, 128], P('pipe', ('seq', 'tp')), may hold values from -24 to 24
- global_blocks: int32 [8, 32, 2], P('pipe', ('seq', 'tp')), may hold values from 0 to 63
- window: int32 [8, 32], P('pipe', ('seq', 'tp')), may hold values from 0 to 1, as said below
- rand_count: int32 [8, 32], P('pipe', ('seq', 'tp')), may hold values from 0 to 3, as said below
- rand_blocks: int32 [8, 32, 64, 3], P('pipe', ('seq', 'tp')), may hold values from 0 to 63
Outputs:
- next_input: bfloat16 [8, 4096, 32, 128], P('pipe', ('seq', 'tp'))
- input_grads: bfloat16 [3, 8, 4096, 32, 128], P(None, 'pipe', ('seq', 'tp'))
Inputs may be any that keep to these rules, and one draw needn't show every extreme that they name: `window`: in every section some head has the half-width 1. `rand_count`: in every section some head has 3 random blocks; most heads have fewer.
All inputs are finite; a program needn't handle non-finite values.
Results may differ from a plain program's by a relative error of at most 0.0085.
Values may be sent and summed in bfloat16 or wider, within the bound.
No kernel may reach another device: no remote copies, remote signals or barrier semaphores. Data moves between devices by JAX's collectives and lax.ppermute only.
A program may use at most 192 MiB of HBM per device.

v0:
```python
import math

import jax
import jax.numpy as jnp
from jax import lax
from jax.experimental import pallas as pl
from jax.experimental.pallas import tpu as pltpu
from jax.sharding import PartitionSpec as P

BLK = 64
GLOBAL = 2
WMAX = 1
R_MOST = 3
SLOTS = 8
HDIM = 128
SCALE = HDIM ** (-0.5)
LOG2E = math.log2(math.e)
MIB = 1 << 20
STEP = 8
QUARTERS = 4
EIGHTHS = 8


def passed_along(value, axis, steps):
    count = lax.axis_size(axis)
    first, last = (max(0, -steps), min(count, count - steps))
    return lax.ppermute(value, axis, [(source, source + steps) for source in range(first, last)])


def key_slots(glob, win, count, rand_ids):
    nblk = rand_ids.shape[0]
    blocks = jnp.arange(nblk, dtype=jnp.int32)[:, None]
    glob_ids = jnp.broadcast_to(glob[None, :], (nblk, GLOBAL))
    glob_open = jnp.ones((nblk, GLOBAL), jnp.bool_)
    offsets = jnp.arange(-WMAX, WMAX + 1, dtype=jnp.int32)[None, :]
    near = blocks + offsets
    near_open = (jnp.abs(offsets) <= win) & (near >= 0) & (near < nblk)
    near = jnp.clip(near, 0, nblk - 1)
    rand_open = jnp.broadcast_to(
        jnp.arange(R_MOST, dtype=jnp.int32)[None, :] < count, (nblk, R_MOST)
    )
    ids = jnp.concatenate([glob_ids, near, rand_ids], axis=1)
    opened = jnp.concatenate([glob_open, near_open, rand_open], axis=1)
    same = ids[:, :, None] == ids[:, None, :]
    earlier = jnp.arange(SLOTS)[None, :] < jnp.arange(SLOTS)[:, None]
    repeated = jnp.any(same & opened[:, None, :] & earlier[None], axis=2)
    return (ids, opened & jnp.logical_not(repeated))


def pack_first_kernel(stage, *refs):
    back, front, out, (wide, heads, sem, out_sem) = refs[:4], refs[4:7], refs[7], refs[8:]
    rows = back[0].shape[0]
    chunks = sem.shape[1]
    size = rows // chunks

    def copy(x, a, c):
        at = pl.ds(c * size, size)
        return pltpu.make_async_copy(x.at[at], wide.at[a, at], sem.at[a, c])

    @pl.when(stage[0] != 0)
    def _():
        for c in range(chunks):
            for a in range(4):
                copy(back[a], a, c).start()

    @pl.when(stage[0] == 0)
    def _():
        for c in range(chunks):
            for a in range(4):
                copy(front[min(a, 2)], a, c).start()

    writes = []
    for c in range(chunks):
        at = pl.ds(c * size, size)
        for a in range(4):
            copy(back[a], a, c).wait()
            heads[:, a, c * size : (c + 1) * size] = jnp.swapaxes(
                wide[a, c * size : (c + 1) * size], 0, 1
            )
        writes.append(pltpu.make_async_copy(heads.at[:, :, at], out.at[:, :, at], out_sem.at[c]))
        writes[-1].start()
    for write in writes:
        write.wait()


def pack_first(stage, back, front):
    rows, heads, hdim = back[0].shape
    return pl.pallas_call(
        pack_first_kernel,
        in_specs=[pl.BlockSpec(memory_space=pltpu.SMEM)]
        + [pl.BlockSpec(memory_space=pl.ANY)] * 7,
        out_specs=pl.BlockSpec(memory_space=pl.ANY),
        out_shape=jax.ShapeDtypeStruct((heads, 4, rows, hdim), jnp.bfloat16),
        scratch_shapes=[
            pltpu.VMEM((4, rows, heads, hdim), jnp.bfloat16),
            pltpu.VMEM((heads, 4, rows, hdim), jnp.bfloat16),
            pltpu.SemaphoreType.DMA((4, 4)),
            pltpu.SemaphoreType.DMA((4,)),
        ],
        compiler_params=pltpu.CompilerParams(vmem_limit_bytes=60 * MIB),
        name="pack_first",
    )(stage, *back, *front)


def pack_rest_kernel(*refs):
    ins, lead, rest = refs[:-2], refs[-2], refs[-1]
    quarter = ins[0].shape[0] // QUARTERS
    for a, x in enumerate(ins):
        heads = jnp.swapaxes(x[...], 0, 1)
        lead[:, a] = heads[:, :-quarter]
        rest[:, a] = heads[:, quarter:]


def pack_rest(arrays):
    rows, heads, hdim = arrays[0].shape
    shape = (heads, len(arrays), rows - rows // QUARTERS, hdim)
    return pl.pallas_call(
        pack_rest_kernel,
        out_shape=[jax.ShapeDtypeStruct(shape, jnp.bfloat16)] * 2,
        compiler_params=pltpu.CompilerParams(vmem_limit_bytes=60 * MIB),
        cost_estimate=pl.CostEstimate(flops=0, bytes_accessed=9 * MIB, transcendentals=0),
        name="pack_rest",
    )(*arrays)


def from_end(stage, stages):
    return jnp.minimum(stage, stages - 1 - stage)


def merge_kernel(size, stage, *refs):
    received, rest, out = refs[:-2], refs[-2], refs[-1]
    f = 0
    for x in received:
        for n in range(x.shape[2] // size):
            to, at = slice(f * size, (f + 1) * size), slice(n * size, (n + 1) * size)

            @pl.when(f < stage[1])
            def _():
                out[:, :, to] = x[:, :, at]

            @pl.when(f >= stage[1])
            def _():
                out[:, :, to] = rest[:, :, to]

            f += 1


def merge(stage, size, received, rest):
    in_vmem = pl.BlockSpec(memory_space=pltpu.VMEM)
    return pl.pallas_call(
        lambda *refs: merge_kernel(size, *refs),
        in_specs=[pl.BlockSpec(memory_space=pltpu.SMEM)] + [in_vmem] * (len(received) + 1),
        out_shape=jax.ShapeDtypeStruct(rest.shape, rest.dtype),
        compiler_params=pltpu.CompilerParams(vmem_limit_bytes=40 * MIB),
        cost_estimate=pl.CostEstimate(flops=0, bytes_accessed=8 * MIB, transcendentals=0),
        name="merge",
    )(stage, *received, rest)


def unpack_kernel(stage, own, late, mixed, out, mixed_out, x, heads, mixed_heads, sem, out_sem):
    steps = out_sem.shape[0] - 1
    size = x.shape[2] // (EIGHTHS - 1)
    rows = heads.shape[1] // steps

    def copy(e):
        at = pl.ds(e * size, size)
        return pltpu.make_async_copy(own.at[:, :, at], x.at[:, :, at], sem.at[e])

    def put(ref, slot, e):
        for a in range(heads.shape[0]):
            heads[a, e * size : (e + 1) * size] = jnp.swapaxes(
                ref[:, a, slot * size : (slot + 1) * size], 0, 1
            )

    for e in range(EIGHTHS - 1):
        pl.when(e < stage[1])(copy(e).start)
    mixed_heads[...] = jnp.swapaxes(mixed[:, 0], 0, 1)
    writes = [pltpu.make_async_copy(mixed_heads, mixed_out.at[0], out_sem.at[steps])]
    writes[-1].start()
    for h in range(steps):
        for e in range(h * EIGHTHS // steps, (h + 1) * EIGHTHS // steps):
            if e < EIGHTHS - 1:

                @pl.when(e < stage[1])
                def _():
                    copy(e).wait()
                    put(x, e, e)

            @pl.when(e >= stage[1])
            def _():
                put(late, max(e - 1, 0), e)

        at = pl.ds(h * rows, rows)
        writes.append(pltpu.make_async_copy(heads.at[:, at], out.at[:, at], out_sem.at[h]))
        writes[-1].start()
    for write in writes:
        write.wait()


def unpack(stage, own, late, mixed):
    heads, count, some, hdim = own.shape
    rows = some * EIGHTHS // (EIGHTHS - 1)
    anywhere = pl.BlockSpec(memory_space=pl.ANY)
    in_vmem = pl.BlockSpec(memory_space=pltpu.VMEM)
    return pl.pallas_call(
        unpack_kernel,
        in_specs=[pl.BlockSpec(memory_space=pltpu.SMEM), anywhere, in_vmem, in_vmem],
        out_specs=[anywhere] * 2,
        out_shape=[
            jax.ShapeDtypeStruct((count, rows, heads, hdim), jnp.bfloat16),
            jax.ShapeDtypeStruct((1, rows, heads, hdim), jnp.bfloat16),
        ],
        scratch_shapes=[
            pltpu.VMEM((heads, count, some, hdim), jnp.bfloat16),
            pltpu.VMEM((count, rows, heads, hdim), jnp.bfloat16),
            pltpu.VMEM((rows, heads, hdim), jnp.bfloat16),
            pltpu.SemaphoreType.DMA((EIGHTHS - 1,)),
            pltpu.SemaphoreType.DMA((4 + 1,)),
        ],
        compiler_params=pltpu.CompilerParams(vmem_limit_bytes=32 * MIB),
        cost_estimate=pl.CostEstimate(flops=0, bytes_accessed=8 * MIB, transcendentals=0),
        name="unpack",
    )(stage, own, late, mixed)


def outward(stages):
    half = stages // 2
    return [(p, p - 1) for p in range(1, half)] + [(p, p + 1) for p in range(half, stages - 1)]


def dot(a, b, dims):
    return lax.dot_general(a, b, (dims, ((), ())), preferred_element_type=jnp.float32)


def block(ref, a, b):
    per = ref.shape[2] // BLK
    return ref[b // per, a, pl.ds(pl.multiple_of((b % per) * BLK, BLK), BLK), :]


def gather(x, a, picks):
    return jnp.concatenate([block(x, a, b) for b in picks], axis=0)


def probabilities(scores, bias):
    scores = [s * (SCALE * LOG2E) + b for s, b in zip(scores, bias)]
    weights = [jnp.exp2(s - jnp.max(s, axis=-1, keepdims=True)) for s in scores]
    return [w * (1.0 / jnp.sum(w, axis=-1, keepdims=True)) for w in weights]


def step_blocks(t, ids, x):
    per = x.shape[2] // BLK
    blocks = [t * STEP + n for n in range(STEP)]
    picks = [[ids[i, c] for c in range(SLOTS)] for i in blocks]
    places = [
        (t * (STEP // per) + n // per, slice((n % per) * BLK, (n % per + 1) * BLK))
        for n in range(STEP)
    ]
    return blocks, picks, places


def forward_kernel(stages, stage, ids, bias, whole, own, back, out, x, sem):
    edge = from_end(stage[0], stages)
    lent = QUARTERS - edge
    quarter = x.shape[2] // QUARTERS

    def copy(ref, f, e):
        return pltpu.make_async_copy(
            ref.at[:, pl.ds(0, x.shape[1]), pl.ds(f * quarter, quarter)],
            x.at[:, :, pl.ds(e * quarter, quarter)],
            sem.at[e],
        )

    for e in range(QUARTERS):
        pl.when(edge == 0)(copy(whole, e, e).start)
        if e < QUARTERS - 1:
            pl.when((edge > 0) & (e < lent))(copy(back, e, e).start)
        if e > 0:
            pl.when((edge > 0) & (e >= lent))(copy(own, e - 1, e).start)
    for e in range(QUARTERS):
        copy(whole, e, e).wait()

    def step(t, carry):
        blocks, picks, places = step_blocks(t, ids, x)
        keys = [gather(x, 1, p) for p in picks]
        values = [gather(x, 2, p) for p in picks]
        queries = [x[j, 0, own, :] for j, own in places]
        scores = [dot(q, k, ((1,), (1,))) for q, k in zip(queries, keys)]
        prob = probabilities(scores, [bias[pl.ds(i, 1), :] for i in blocks])
        prob = [p.astype(jnp.bfloat16) for p in prob]
        for (j, own), p, v in zip(places, prob, values):
            out[j, 0, own, :] = dot(p, v, ((1,), (0,))).astype(jnp.bfloat16)
        return carry

    lax.fori_loop(0, ids.shape[0] // STEP, step, 0)


def backward_kernel(stages, stage, ids, bias, x, lead, last, rest, dk, dv):
    del stages, stage
    parts, _, rows, hdim = x.shape
    size = rows // EIGHTHS
    ranges = [(lead, 0), (last, rows - 2 * size), (rest, size)]

    def put(j, a, at, rows_of):
        count = rows_of.shape[-2]
        for out, start in ranges:
            low, high = max(at, start), min(at + count, start + out.shape[2])
            if low < high:
                out[j, a, low - start : high - start, :] = rows_of[..., low - at : high - at, :]

    dk[...] = jnp.zeros_like(dk)
    dv[...] = jnp.zeros_like(dv)

    def step(t, carry):
        blocks, picks, places = step_blocks(t, ids, x)
        keys = [gather(x, 1, p) for p in picks]
        values = [gather(x, 2, p) for p in picks]
        queries = [x[j, 0, own, :] for j, own in places]
        grads = [x[j, 3, own, :] for j, own in places]
        scores = [dot(q, k, ((1,), (1,))) for q, k in zip(queries, keys)]
        dprob = [dot(g, v, ((1,), (1,))) for g, v in zip(grads, values)]
        prob = probabilities(scores, [bias[pl.ds(i, 1), :] for i in blocks])
        prob_b = [p.astype(jnp.bfloat16) for p in prob]
        value_part = [dot(p, g, ((0,), (0,))) for p, g in zip(prob_b, grads)]
        delta = [
            jnp.sum(p.astype(jnp.float32) * d, axis=-1, keepdims=True)
            for p, d in zip(prob_b, dprob)
        ]
        dscore = [
            (p * ((d - e) * SCALE)).astype(jnp.bfloat16) for p, d, e in zip(prob, dprob, delta)
        ]
        key_part = [dot(d, q, ((0,), (0,))) for d, q in zip(dscore, queries)]
        for (j, own), d, k in zip(places, dscore, keys):
            put(j, 0, own.start, dot(d, k, ((1,), (0,))).astype(jnp.bfloat16))
        for pick, kp, vp in zip(picks, key_part, value_part):
            for c, b in enumerate(pick):
                at = pl.ds(pl.multiple_of(b * BLK, BLK), BLK)
                dk[at, :] += kp[c * BLK : (c + 1) * BLK]
                dv[at, :] += vp[c * BLK : (c + 1) * BLK]
        return carry

    lax.fori_loop(0, ids.shape[0] // STEP, step, 0)
    put(slice(None), 1, 0, dk[...].reshape(parts, rows, hdim).astype(jnp.bfloat16))
    put(slice(None), 2, 0, dv[...].reshape(parts, rows, hdim).astype(jnp.bfloat16))


def attention(kernel, results, lengths, stage, ids, bias, ins, rest, scratch, matmuls):
    parts, _, rows, hdim = (*ins, *rest)[0].shape
    work = parts * rows * SLOTS * BLK * hdim * 2
    stages = lax.axis_size("pipe")
    in_smem = pl.BlockSpec(memory_space=pltpu.SMEM)
    in_vmem = pl.BlockSpec(memory_space=pltpu.VMEM)
    return pl.pallas_call(
        lambda *refs: kernel(stages, *refs),
        out_shape=[
            jax.ShapeDtypeStruct((parts, results, n, hdim), jnp.bfloat16) for n in lengths
        ],
        in_specs=[in_smem, in_smem, in_vmem]
        + [in_vmem] * len(ins)
        + [pl.BlockSpec(memory_space=pl.ANY)] * len(rest),
        scratch_shapes=scratch,
        compiler_params=pltpu.CompilerParams(vmem_limit_bytes=(40 if ins else 60) * MIB),
        cost_estimate=pl.CostEstimate(
            flops=4 * matmuls * work, bytes_accessed=8 * MIB, transcendentals=0
        ),
        name=kernel.__name__,
    )(stage, ids, bias, *ins, *rest)


def exchange(x):
    return lax.all_to_all(x, ("seq", "tp"), split_axis=0, concat_axis=0, tiled=True)


def slots_and_bias(glob, win, count, rand_ids):
    ids, opened = key_slots(glob, win, count, rand_ids)
    bias = jnp.where(jnp.repeat(opened, BLK, axis=1), 0.0, -1e30).astype(jnp.float32)
    return ids, bias


def body(
    query_fwd,
    key_fwd,
    value_fwd,
    query_bwd,
    key_bwd,
    value_bwd,
    grad_mix,
    global_blocks,
    window,
    rand_count,
    rand_blocks,
):
    ids, bias = slots_and_bias(
        global_blocks[0, 0], window[0, 0], rand_count[0, 0], rand_blocks[0, 0]
    )
    stages = lax.axis_size("pipe")
    stage = lax.axis_index("pipe").astype(jnp.int32)[None]
    front = (query_fwd[0], key_fwd[0], value_fwd[0])
    first = exchange(
        pack_first(stage, (query_bwd[0], key_bwd[0], value_bwd[0], grad_mix[0]), front)
    )
    lead, rest = pack_rest(front)
    received = lax.ppermute(lead, "pipe", outward(stages))
    parts, _, rows, _ = first.shape
    quarter, eighth = rows // QUARTERS, rows // EIGHTHS
    lent = jnp.concatenate([stage, QUARTERS - 1 - from_end(stage, stages)])
    second = merge(lent, quarter, [received], rest)
    second, ids, bias = lax.optimization_barrier((second, ids, bias))
    second = exchange(second)
    early, last, rest = attention(
        backward_kernel, 3, [rows - 2 * eighth, eighth, rows - eighth],
        stage, ids, bias, [first], [], [pltpu.VMEM((parts * rows, HDIM), jnp.float32)] * 2, 5,
    )
    early = passed_along(early, "pipe", -1)
    last = lax.ppermute(last, "pipe", [(1, 0)])
    lent = jnp.concatenate([stage, EIGHTHS - 1 - stage])
    grads = merge(lent, eighth, [early, last], rest)
    back = lax.ppermute(second, "pipe", [(b, a) for a, b in outward(stages)])
    (mixed,) = attention(
        forward_kernel, 1, [rows], stage, ids, bias, [], [first, second, back],
        [
            pltpu.VMEM((parts, 3, rows, HDIM), jnp.bfloat16),
            pltpu.SemaphoreType.DMA((QUARTERS,)),
        ],
        2,
    )
    mixed = passed_along(mixed, "pipe", 1)
    grads = exchange(grads)
    late = passed_along(grads, "pipe", -1)
    mixed = exchange(mixed)
    grads, mixed = unpack(lent, grads, late, mixed)
    return (mixed, grads[:, None])


def solution(mesh):
    rows = P("pipe", ("seq", "tp"), None, None)
    placed = (rows,) * 7 + (
        P("pipe", ("seq", "tp"), None),
        P("pipe", ("seq", "tp")),
        P("pipe", ("seq", "tp")),
        P("pipe", ("seq", "tp"), None, None),
    )
    return jax.shard_map(
        body,
        mesh=mesh,
        in_specs=placed,
        out_specs=(rows, P(None, "pipe", ("seq", "tp"), None, None)),
        check_vma=False,
    )
```

profile of v0, /device:TPU:1, one launch (start us, length us, event | category | flops | bytes accessed | tf_op | source)
XLA Modules:
  0.0 284.2 jit_solution(10991133433287705473)
XLA Ops:
  0.6 3.5 %pack_first.1 = bf16[32,4,128,128]{3,2,1,0:T(8,128)(2,1)} custom-call(s32[1]{0:T(128)} %bitcast.stage.refs_0_, bf16[128,32,128]{2,1,0:T(8,128)(2,1)} %bitcast.25, bf16[128,32,128]{2,1,0:T(8,128)(2,1)} %bitcast.26, bf16[128,32,128]{2,1,0:T(8,128)(2,1)} %bitcast.27, bf16[128,32,128]{2,1,0:T(8,128)(2,1)} %bitcast.28, bf16[128,32,128]{2,1,0:T(8,128)(2,1)} %bitcast.19, ...), custom_call_target="tpu_custom_call" | custom-call | tf_op jit(solution)/shard_map/pack_first/pallas_call | solution.py:88
  4.2 12.2 %all-to-all-start = ((bf16[32,4,128,128]{3,2,1,0:T(8,128)(2,1)}), bf16[32,4,128,128]{3,2,1,0:T(8,128)(2,1)}, u32[]{:S(2)}, u32[]{:S(2)}) async-start(bf16[32,4,128,128]{3,2,1,0:T(8,128)(2,1)} %pack_first.1), calls=%async_computation | async-start | bytes 8388608 | tf_op jit(solution)/shard_map/all_to_all | solution.py:370
  16.4 5.1 %pack_rest.1 = (bf16[32,3,96,128]{3,2,1,0:T(8,128)(2,1)}, bf16[32,3,96,128]{3,2,1,0:T(8,128)(2,1)}) custom-call(bf16[128,32,128]{2,1,0:T(8,128)(2,1)} %bitcast.20, bf16[128,32,128]{2,1,0:T(8,128)(2,1)} %bitcast.22, bf16[128,32,128]{2,1,0:T(8,128)(2,1)} %bitcast.24), custom_call_target="tpu_custom_call" | custom-call | bytes 9437184 | tf_op jit(solution)/shard_map/pack_rest/pallas_call | solution.py:117
  21.5 3.7 %collective-permute-start = (bf16[32,3,96,128]{3,2,1,0:T(8,128)(2,1)}, bf16[32,3,96,128]{3,2,1,0:T(8,128)(2,1)S(1)}, u32[]{:S(2)}, u32[]{:S(2)}) collective-permute-start(bf16[32,3,96,128]{3,2,1,0:T(8,128)(2,1)} %get-tuple-element.12), channel_id=1, source_target_pairs={{32,0},{64,32},{96,64},{128,160},{160,192},{192,224},{33,1},{65,33... | collective-permute-start | bytes 7077896 | tf_op jit(solution)/shard_map/ppermute | solution.py:402
  26.8 0.1 add_add_fusion
  27.0 0.1 and_reduce_fusion
  27.1 0.1 and_select_fusion
  27.2 0.1 copy.22
  27.2 0.1 broadcast_in_dim.48
  27.4 0.1 select_n.9.refs_2_
  27.6 25.0 %collective-permute-done.refs_1_ = bf16[32,3,96,128]{3,2,1,0:T(8,128)(2,1)S(1)} collective-permute-done((bf16[32,3,96,128]{3,2,1,0:T(8,128)(2,1)}, bf16[32,3,96,128]{3,2,1,0:T(8,128)(2,1)S(1)}, u32[]{:S(2)}, u32[]{:S(2)}) %collective-permute-start) | collective-permute-done | bytes 2359328 | tf_op jit(solution)/shard_map/ppermute | solution.py:402
  52.6 1.7 copy-done.1
  54.2 2.2 merge.2
  56.4 52.2 %all-to-all-done.refs_3_ = bf16[32,4,128,128]{3,2,1,0:T(8,128)(2,1)} async-done(((bf16[32,4,128,128]{3,2,1,0:T(8,128)(2,1)}), bf16[32,4,128,128]{3,2,1,0:T(8,128)(2,1)}, u32[]{:S(2)}, u32[]{:S(2)}) %all-to-all-start) | async-done | bytes 4194336 | tf_op jit(solution)/shard_map/all_to_all | solution.py:370
  108.7 7.8 %all-to-all-start.2 = ((bf16[32,3,96,128]{3,2,1,0:T(8,128)(2,1)}), bf16[32,3,96,128]{3,2,1,0:T(8,128)(2,1)}, u32[]{:S(2)}, u32[]{:S(2)}) async-start(bf16[32,3,96,128]{3,2,1,0:T(8,128)(2,1)} %merge.2), calls=%async_computation.2 | async-start | bytes 4718592 | tf_op jit(solution)/shard_map/all_to_all | solution.py:370
  116.5 0.1 copy.23.refs_1_
  116.6 19.4 %backward_kernel.1 = (bf16[32,3,96,128]{3,2,1,0:T(8,128)(2,1)S(1)}, bf16[32,3,16,128]{3,2,1,0:T(8,128)(2,1)S(1)}, bf16[32,3,112,128]{3,2,1,0:T(8,128)(2,1)S(1)}) custom-call(s32[1]{0:T(128)} %bitcast.stage.refs_0_, s32[64,8]{1,0:T(8,128)S(1)} %copy.23.refs_1_, f32[64,512]{1,0:T(8,128)S(1)} %select_n.9.refs_2_, bf16[32,4,128,128]{3,2,1,0:T(8,128)(2,1)} %all-to-all-done.refs_3_), custom_call_target="tpu_custom_call" | custom-call | flops 10737418240 | bytes 8388608 | tf_op jit(solution)/shard_map/backward_kernel/pallas_call | solution.py:352
  136.0 4.0 %collective-permute-start.1 = (bf16[32,3,96,128]{3,2,1,0:T(8,128)(2,1)S(1)}, bf16[32,3,96,128]{3,2,1,0:T(8,128)(2,1)S(1)}, u32[]{:S(2)}, u32[]{:S(2)}) collective-permute-start(bf16[32,3,96,128]{3,2,1,0:T(8,128)(2,1)S(1)} %get-tuple-element.16), channel_id=1, source_target_pairs={{32,0},{64,32},{96,64},{128,96},{160,128},{192,160},{224,192},{33,... | collective-permute-start | bytes 7077896 | tf_op jit(solution)/shard_map/ppermute | solution.py:27
  140.0 1.3 collective-permute-start.2
  141.4 3.3 %collective-permute-done.2.refs_2_ = bf16[32,3,16,128]{3,2,1,0:T(8,128)(2,1)S(1)} collective-permute-done((bf16[32,3,16,128]{3,2,1,0:T(8,128)(2,1)S(1)}, bf16[32,3,16,128]{3,2,1,0:T(8,128)(2,1)S(1)}, u32[]{:S(2)}, u32[]{:S(2)}) %collective-permute-start.2) | collective-permute-done | bytes 393248 | tf_op jit(solution)/shard_map/ppermute | solution.py:414
  144.7 23.4 %collective-permute-done.1.refs_1_ = bf16[32,3,96,128]{3,2,1,0:T(8,128)(2,1)S(1)} collective-permute-done((bf16[32,3,96,128]{3,2,1,0:T(8,128)(2,1)S(1)}, bf16[32,3,96,128]{3,2,1,0:T(8,128)(2,1)S(1)}, u32[]{:S(2)}, u32[]{:S(2)}) %collective-permute-start.1) | collective-permute-done | bytes 2359328 | tf_op jit(solution)/shard_map/ppermute | solution.py:27
  168.0 0.8 merge.3
  168.9 1.5 copy-done
  170.4 9.4 %all-to-all-start.1 = ((bf16[32,3,112,128]{3,2,1,0:T(8,128)(2,1)}), bf16[32,3,112,128]{3,2,1,0:T(8,128)(2,1)S(1)}, u32[]{:S(2)}, u32[]{:S(2)}) async-start(bf16[32,3,112,128]{3,2,1,0:T(8,128)(2,1)} %copy-done), calls=%async_computation.1 | async-start | bytes 5505024 | tf_op jit(solution)/shard_map/all_to_all | solution.py:370
  179.8 3.1 %collective-permute-start.4 = (bf16[32,3,96,128]{3,2,1,0:T(8,128)(2,1)}, bf16[32,3,96,128]{3,2,1,0:T(8,128)(2,1)}, u32[]{:S(2)}, u32[]{:S(2)}) collective-permute-start(bf16[32,3,96,128]{3,2,1,0:T(8,128)(2,1)} %all-to-all-done.2.refs_4_), channel_id=1, source_target_pairs={{0,32},{32,64},{64,96},{160,128},{192,160},{224,192},{1,33},{33,65... | collective-permute-start | bytes 7077896 | tf_op jit(solution)/shard_map/ppermute | solution.py:417
  182.9 26.1 %collective-permute-done.4.refs_5_ = bf16[32,3,96,128]{3,2,1,0:T(8,128)(2,1)} collective-permute-done((bf16[32,3,96,128]{3,2,1,0:T(8,128)(2,1)}, bf16[32,3,96,128]{3,2,1,0:T(8,128)(2,1)}, u32[]{:S(2)}, u32[]{:S(2)}) %collective-permute-start.4) | collective-permute-done | bytes 2359328 | tf_op jit(solution)/shard_map/ppermute | solution.py:417
  209.0 12.3 %forward_kernel.1 = bf16[32,1,128,128]{3,2,1,0:T(8,128)(2,1)} custom-call(s32[1]{0:T(128)} %bitcast.stage.refs_0_, s32[64,8]{1,0:T(8,128)} %copy-done.3, f32[64,512]{1,0:T(8,128)} %copy-done.2, bf16[32,4,128,128]{3,2,1,0:T(8,128)(2,1)} %all-to-all-done.refs_3_, bf16[32,3,96,128]{3,2,1,0:T(8,128)(2,1)} %all-to-all-done.2.refs_4_, ...), custom_call_target="tpu_custom_call" | custom-call | flops 4294967296 | bytes 8388608 | tf_op jit(solution)/shard_map/forward_kernel/pallas_call | solution.py:352
  221.3 4.4 %collective-permute-start.5 = (bf16[32,1,128,128]{3,2,1,0:T(8,128)(2,1)}, bf16[32,1,128,128]{3,2,1,0:T(8,128)(2,1)}, u32[]{:S(2)}, u32[]{:S(2)}) collective-permute-start(bf16[32,1,128,128]{3,2,1,0:T(8,128)(2,1)} %forward_kernel.1), channel_id=1, source_target_pairs={{0,32},{32,64},{64,96},{96,128},{128,160},{160,192},{192,224},{1,3... | collective-permute-start | bytes 3145736 | tf_op jit(solution)/shard_map/ppermute | solution.py:27
  225.7 19.7 %all-to-all-done.1.own = bf16[32,3,112,128]{3,2,1,0:T(8,128)(2,1)S(1)} async-done(((bf16[32,3,112,128]{3,2,1,0:T(8,128)(2,1)}), bf16[32,3,112,128]{3,2,1,0:T(8,128)(2,1)S(1)}, u32[]{:S(2)}, u32[]{:S(2)}) %all-to-all-start.1) | async-done | bytes 2752544 | tf_op jit(solution)/shard_map/all_to_all | solution.py:370
  245.4 2.3 collective-permute-start.3
  247.7 33.3 %all_to_all.20.mixed = bf16[32,1,128,128]{3,2,1,0:T(8,128)(2,1)S(1)} all-to-all(bf16[32,1,128,128]{3,2,1,0:T(8,128)(2,1)} %collective-permute-done.5), channel_id=1, replica_groups=mesh['pipe'=8,'seq'=8,'tp'=4] {'seq','tp'}, dimensions={0} | all-to-all | bytes 2097152 | tf_op jit(solution)/shard_map/all_to_all | solution.py:370
  281.0 3.2 %unpack.1 = (bf16[3,128,32,128]{3,2,1,0:T(8,128)(2,1)}, bf16[1,128,32,128]{3,2,1,0:T(8,128)(2,1)}) custom-call(s32[2]{0:T(128)S(1)} %pad_add_fusion.1.refs_0_.stage, bf16[32,3,112,128]{3,2,1,0:T(8,128)(2,1)S(1)} %all-to-all-done.1.own, bf16[32,3,112,128]{3,2,1,0:T(8,128)(2,1)S(1)} %collective-permute-done.3.late, bf16[32,1,128,128]{3,2,1,0:T(8,128)(2,1)S(1)} %all_to_all.20.mixed), custom_call_target="tpu_custom_call" | custom-call | bytes 8388608 | tf_op jit(solution)/shard_map/unpack/pallas_call | solution.py:205
  (27 shorter events, 0.5 us)
Async XLA Ops:
  4.2 104.5 %all-to-all-start = ((bf16[32,4,128,128]{3,2,1,0:T(8,128)(2,1)}), bf16[32,4,128,128]{3,2,1,0:T(8,128)(2,1)}, u32[]{:S(2)}, u32[]{:S(2)}) async-start(bf16[32,4,128,128]{3,2,1,0:T(8,128)(2,1)} %pack_first.1), calls=%async_computation | async-start | bytes 8388608 | tf_op jit(solution)/shard_map/all_to_all | solution.py:370
  16.4 10.2 %copy-start.4 = (s32[1,1,64,3]{2,1,3,0:T(1,128)S(1)}, s32[1,1,64,3]{2,1,3,0:T(1,128)}, u32[]{:S(2)}) copy-start(s32[1,1,64,3]{2,1,3,0:T(1,128)} %param.21) | copy-start | bytes 2308
  16.4 10.2 %copy-start.5 = (s32[1,1,2]{2,1,0:T(1,128)S(1)}, s32[1,1,2]{2,1,0:T(1,128)}, u32[]{:S(2)}) copy-start(s32[1,1,2]{2,1,0:T(1,128)} %param.18) | copy-start | bytes 28
  21.5 31.1 %collective-permute-start = (bf16[32,3,96,128]{3,2,1,0:T(8,128)(2,1)}, bf16[32,3,96,128]{3,2,1,0:T(8,128)(2,1)S(1)}, u32[]{:S(2)}, u32[]{:S(2)}) collective-permute-start(bf16[32,3,96,128]{3,2,1,0:T(8,128)(2,1)} %get-tuple-element.12), channel_id=1, source_target_pairs={{32,0},{64,32},{96,64},{128,160},{160,192},{192,224},{33,1},{65,33... | collective-permute-start | bytes 7077896 | tf_op jit(solution)/shard_map/ppermute | solution.py:402
  27.5 89.1 %copy-start.2 = (f32[64,512]{1,0:T(8,128)}, f32[64,512]{1,0:T(8,128)S(1)}, u32[]{:S(2)}) copy-start(f32[64,512]{1,0:T(8,128)S(1)} %select_n.9.refs_2_) | copy-start | bytes 393220
  52.6 1.7 copy-start.1
  108.7 61.7 %all-to-all-start.2 = ((bf16[32,3,96,128]{3,2,1,0:T(8,128)(2,1)}), bf16[32,3,96,128]{3,2,1,0:T(8,128)(2,1)}, u32[]{:S(2)}, u32[]{:S(2)}) async-start(bf16[32,3,96,128]{3,2,1,0:T(8,128)(2,1)} %merge.2), calls=%async_computation.2 | async-start | bytes 4718592 | tf_op jit(solution)/shard_map/all_to_all | solution.py:370
  116.6 19.4 %copy-start.3 = (s32[64,8]{1,0:T(8,128)}, s32[64,8]{1,0:T(8,128)S(1)}, u32[]{:S(2)}) copy-start(s32[64,8]{1,0:T(8,128)S(1)} %copy.23.refs_1_) | copy-start | bytes 6148
  136.0 32.0 %collective-permute-start.1 = (bf16[32,3,96,128]{3,2,1,0:T(8,128)(2,1)S(1)}, bf16[32,3,96,128]{3,2,1,0:T(8,128)(2,1)S(1)}, u32[]{:S(2)}, u32[]{:S(2)}) collective-permute-start(bf16[32,3,96,128]{3,2,1,0:T(8,128)(2,1)S(1)} %get-tuple-element.16), channel_id=1, source_target_pairs={{32,0},{64,32},{96,64},{128,96},{160,128},{192,160},{224,192},{33,... | collective-permute-start | bytes 7077896 | tf_op jit(solution)/shard_map/ppermute | solution.py:27
  140.0 4.7 %collective-permute-start.2 = (bf16[32,3,16,128]{3,2,1,0:T(8,128)(2,1)S(1)}, bf16[32,3,16,128]{3,2,1,0:T(8,128)(2,1)S(1)}, u32[]{:S(2)}, u32[]{:S(2)}) collective-permute-start(bf16[32,3,16,128]{3,2,1,0:T(8,128)(2,1)S(1)} %get-tuple-element.17), channel_id=1, source_target_pairs={{32,0},{33,1},{34,2},{35,3},{36,4},{37,5},{38,6},{39,7},{40,8},{41... | collective-permute-start | bytes 1179656 | tf_op jit(solution)/shard_map/ppermute | solution.py:414
  168.9 1.5 copy-start
  170.4 75.0 %all-to-all-start.1 = ((bf16[32,3,112,128]{3,2,1,0:T(8,128)(2,1)}), bf16[32,3,112,128]{3,2,1,0:T(8,128)(2,1)S(1)}, u32[]{:S(2)}, u32[]{:S(2)}) async-start(bf16[32,3,112,128]{3,2,1,0:T(8,128)(2,1)} %copy-done), calls=%async_computation.1 | async-start | bytes 5505024 | tf_op jit(solution)/shard_map/all_to_all | solution.py:370
  179.8 29.2 %collective-permute-start.4 = (bf16[32,3,96,128]{3,2,1,0:T(8,128)(2,1)}, bf16[32,3,96,128]{3,2,1,0:T(8,128)(2,1)}, u32[]{:S(2)}, u32[]{:S(2)}) collective-permute-start(bf16[32,3,96,128]{3,2,1,0:T(8,128)(2,1)} %all-to-all-done.2.refs_4_), channel_id=1, source_target_pairs={{0,32},{32,64},{64,96},{160,128},{192,160},{224,192},{1,33},{33,65... | collective-permute-start | bytes 7077896 | tf_op jit(solution)/shard_map/ppermute | solution.py:417
  221.3 26.4 %collective-permute-start.5 = (bf16[32,1,128,128]{3,2,1,0:T(8,128)(2,1)}, bf16[32,1,128,128]{3,2,1,0:T(8,128)(2,1)}, u32[]{:S(2)}, u32[]{:S(2)}) collective-permute-start(bf16[32,1,128,128]{3,2,1,0:T(8,128)(2,1)} %forward_kernel.1), channel_id=1, source_target_pairs={{0,32},{32,64},{64,96},{96,128},{128,160},{160,192},{192,224},{1,3... | collective-permute-start | bytes 3145736 | tf_op jit(solution)/shard_map/ppermute | solution.py:27
  245.4 35.6 %collective-permute-start.3 = (bf16[32,3,112,128]{3,2,1,0:T(8,128)(2,1)S(1)}, bf16[32,3,112,128]{3,2,1,0:T(8,128)(2,1)S(1)}, u32[]{:S(2)}, u32[]{:S(2)}) collective-permute-start(bf16[32,3,112,128]{3,2,1,0:T(8,128)(2,1)S(1)} %all-to-all-done.1.own), channel_id=1, source_target_pairs={{32,0},{64,32},{96,64},{128,96},{160,128},{192,160},{224,192},{33,... | collective-permute-start | bytes 8257544 | tf_op jit(solution)/shard_map/ppermute | solution.py:27
where the time goes:
time: 285 us; the launch traced here: 284 us
  waiting for transfers between devices  150 us (53%)
  starting transfers between devices  48.1 us (17%)
  Pallas kernels  46.5 us (16%)
  blocking collectives  33.3 us (12%)
  local copies, waits for them, and re-layouts  3.72 us (1%)
    all_to_all x3, waiting for transfers between devices, exchange(): lax.all_to_all(x, ('seq', 'tp'), split_axis=0, concat_axis=0, tiled=True)  71.9 us
    all_to_all x1, blocking collectives, exchange(): lax.all_to_all(x, ('seq', 'tp'), split_axis=0, concat_axis=0, tiled=True)  33.3 us
    pallas_call x2, Pallas kernels, attention(): pl.pallas_call(lambda *refs: kernel(stages, *refs), out_shape=[jax.ShapeD...  31.7 us
    all_to_all x3, starting transfers between devices, exchange(): lax.all_to_all(x, ('seq', 'tp'), split_axis=0, concat_axis=0, tiled=True)  29.4 us
    ppermute x1, waiting for transfers between devices, body(): back = lax.ppermute(second, 'pipe', [(b, a) for a, b in outward(stages)])  26.1 us
    ppermute x1, waiting for transfers between devices, body(): received = lax.ppermute(lead, 'pipe', outward(stages))  25 us
    ppermute x3, waiting for transfers between devices, passed_along(): lax.ppermute(value, axis, [(source, source + steps) for source in range(f...  23.4 us
    ppermute x3, starting transfers between devices, passed_along(): lax.ppermute(value, axis, [(source, source + steps) for source in range(f...  10.6 us
  transfers between devices with their start and end apart: 9, of which 6 were waited for; matrix products, arithmetic and copies ran while one was open for 0% of the time, Pallas kernels for 14%

commit v1 on v0

--- a/solution.py
+++ b/solution.py
@@ -16,7 +16,7 @@
 SCALE = HDIM ** (-0.5)
 LOG2E = math.log2(math.e)
 MIB = 1 << 20
-STEP = 8
+STEP = 16
 QUARTERS = 4
 EIGHTHS = 8
 

time: 285 us -> 284 us (level)
  starting transfers between devices: 48.1 us -> 51.2 us
  transfers between devices with their start and end apart: 9 -> 9, of which waited for: 6 -> 6; matrix products, arithmetic and copies ran while one was open for 0% -> 0% of each run, Pallas kernels for 14% -> 13%
where the time goes in v1:
time: 284 us
  waiting for transfers between devices  148 us (52%)
  starting transfers between devices  51.2 us (18%)
  Pallas kernels  44.2 us (16%)
  blocking collectives  33.3 us (12%)
  local copies, waits for them, and re-layouts  3.72 us (1%)
    all_to_all x3, waiting for transfers between devices, exchange(): lax.all_to_all(x, ('seq', 'tp'), split_axis=0, concat_axis=0, tiled=True)  70.7 us
    all_to_all x1, blocking collectives, exchange(): lax.all_to_all(x, ('seq', 'tp'), split_axis=0, concat_axis=0, tiled=True)  33.3 us
    all_to_all x3, starting transfers between devices, exchange(): lax.all_to_all(x, ('seq', 'tp'), split_axis=0, concat_axis=0, tiled=True)  29.4 us
    pallas_call x2, Pallas kernels, attention(): pl.pallas_call(lambda *refs: kernel(stages, *refs), out_shape=[jax.ShapeD...  29.4 us
    ppermute x1, waiting for transfers between devices, body(): back = lax.ppermute(second, 'pipe', [(b, a) for a, b in outward(stages)])  25.9 us
    ppermute x1, waiting for transfers between devices, body(): received = lax.ppermute(lead, 'pipe', outward(stages))  25 us
    ppermute x3, waiting for transfers between devices, passed_along(): lax.ppermute(value, axis, [(source, source + steps) for source in range(f...  23.3 us
    ppermute x3, starting transfers between devices, passed_along(): lax.ppermute(value, axis, [(source, source + steps) for source in range(f...  12.8 us
  transfers between devices with their start and end apart: 9, of which 6 were waited for; matrix products, arithmetic and copies ran while one was open for 0% of the time, Pallas kernels for 13%

profile of v1, /device:TPU:1, one launch (start us, length us, event | category | flops | bytes accessed | tf_op | source)
XLA Modules:
  0.0 283.6 jit_solution(16366723700986378486)
XLA Ops:
  0.6 3.5 %pack_first.1 = bf16[32,4,128,128]{3,2,1,0:T(8,128)(2,1)} custom-call(s32[1]{0:T(128)} %bitcast.stage.refs_0_, bf16[128,32,128]{2,1,0:T(8,128)(2,1)} %bitcast.25, bf16[128,32,128]{2,1,0:T(8,128)(2,1)} %bitcast.26, bf16[128,32,128]{2,1,0:T(8,128)(2,1)} %bitcast.27, bf16[128,32,128]{2,1,0:T(8,128)(2,1)} %bitcast.28, bf16[128,32,128]{2,1,0:T(8,128)(2,1)} %bitcast.19, ...), custom_call_target="tpu_custom_call" | custom-call | tf_op jit(solution)/shard_map/pack_first/pallas_call | solution.py:88
  4.2 12.2 %all-to-all-start = ((bf16[32,4,128,128]{3,2,1,0:T(8,128)(2,1)}), bf16[32,4,128,128]{3,2,1,0:T(8,128)(2,1)}, u32[]{:S(2)}, u32[]{:S(2)}) async-start(bf16[32,4,128,128]{3,2,1,0:T(8,128)(2,1)} %pack_first.1), calls=%async_computation | async-start | bytes 8388608 | tf_op jit(solution)/shard_map/all_to_all | solution.py:370
  16.4 5.1 %pack_rest.1 = (bf16[32,3,96,128]{3,2,1,0:T(8,128)(2,1)}, bf16[32,3,96,128]{3,2,1,0:T(8,128)(2,1)}) custom-call(bf16[128,32,128]{2,1,0:T(8,128)(2,1)} %bitcast.20, bf16[128,32,128]{2,1,0:T(8,128)(2,1)} %bitcast.22, bf16[128,32,128]{2,1,0:T(8,128)(2,1)} %bitcast.24), custom_call_target="tpu_custom_call" | custom-call | bytes 9437184 | tf_op jit(solution)/shard_map/pack_rest/pallas_call | solution.py:117
  21.5 3.7 %collective-permute-start = (bf16[32,3,96,128]{3,2,1,0:T(8,128)(2,1)}, bf16[32,3,96,128]{3,2,1,0:T(8,128)(2,1)S(1)}, u32[]{:S(2)}, u32[]{:S(2)}) collective-permute-start(bf16[32,3,96,128]{3,2,1,0:T(8,128)(2,1)} %get-tuple-element.12), channel_id=1, source_target_pairs={{32,0},{64,32},{96,64},{128,160},{160,192},{192,224},{33,1},{65,33... | collective-permute-start | bytes 7077896 | tf_op jit(solution)/shard_map/ppermute | solution.py:402
  26.8 0.1 add_add_fusion
  27.0 0.1 and_reduce_fusion
  27.1 0.1 and_select_fusion
  27.2 0.1 copy.22
  27.2 0.1 broadcast_in_dim.48
  27.4 0.1 select_n.9.refs_2_
  27.6 25.0 %collective-permute-done.refs_1_ = bf16[32,3,96,128]{3,2,1,0:T(8,128)(2,1)S(1)} collective-permute-done((bf16[32,3,96,128]{3,2,1,0:T(8,128)(2,1)}, bf16[32,3,96,128]{3,2,1,0:T(8,128)(2,1)S(1)}, u32[]{:S(2)}, u32[]{:S(2)}) %collective-permute-start) | collective-permute-done | bytes 2359328 | tf_op jit(solution)/shard_map/ppermute | solution.py:402
  52.6 1.7 copy-done.1
  54.2 2.2 merge.2
  56.4 52.2 %all-to-all-done.refs_3_ = bf16[32,4,128,128]{3,2,1,0:T(8,128)(2,1)} async-done(((bf16[32,4,128,128]{3,2,1,0:T(8,128)(2,1)}), bf16[32,4,128,128]{3,2,1,0:T(8,128)(2,1)}, u32[]{:S(2)}, u32[]{:S(2)}) %all-to-all-start) | async-done | bytes 4194336 | tf_op jit(solution)/shard_map/all_to_all | solution.py:370
  108.7 7.8 %all-to-all-start.2 = ((bf16[32,3,96,128]{3,2,1,0:T(8,128)(2,1)}), bf16[32,3,96,128]{3,2,1,0:T(8,128)(2,1)}, u32[]{:S(2)}, u32[]{:S(2)}) async-start(bf16[32,3,96,128]{3,2,1,0:T(8,128)(2,1)} %merge.2), calls=%async_computation.2 | async-start | bytes 4718592 | tf_op jit(solution)/shard_map/all_to_all | solution.py:370
  116.5 0.1 copy.23.refs_1_
  116.6 18.7 %backward_kernel.1 = (bf16[32,3,96,128]{3,2,1,0:T(8,128)(2,1)S(1)}, bf16[32,3,16,128]{3,2,1,0:T(8,128)(2,1)S(1)}, bf16[32,3,112,128]{3,2,1,0:T(8,128)(2,1)S(1)}) custom-call(s32[1]{0:T(128)} %bitcast.stage.refs_0_, s32[64,8]{1,0:T(8,128)S(1)} %copy.23.refs_1_, f32[64,512]{1,0:T(8,128)S(1)} %select_n.9.refs_2_, bf16[32,4,128,128]{3,2,1,0:T(8,128)(2,1)} %all-to-all-done.refs_3_), custom_call_target="tpu_custom_call" | custom-call | flops 10737418240 | bytes 8388608 | tf_op jit(solution)/shard_map/backward_kernel/pallas_call | solution.py:352
  135.3 4.0 %collective-permute-start.1 = (bf16[32,3,96,128]{3,2,1,0:T(8,128)(2,1)S(1)}, bf16[32,3,96,128]{3,2,1,0:T(8,128)(2,1)S(1)}, u32[]{:S(2)}, u32[]{:S(2)}) collective-permute-start(bf16[32,3,96,128]{3,2,1,0:T(8,128)(2,1)S(1)} %get-tuple-element.16), channel_id=1, source_target_pairs={{32,0},{64,32},{96,64},{128,96},{160,128},{192,160},{224,192},{33,... | collective-permute-start | bytes 7077896 | tf_op jit(solution)/shard_map/ppermute | solution.py:27
  139.2 1.3 collective-permute-start.2
  140.6 3.3 %collective-permute-done.2.refs_2_ = bf16[32,3,16,128]{3,2,1,0:T(8,128)(2,1)S(1)} collective-permute-done((bf16[32,3,16,128]{3,2,1,0:T(8,128)(2,1)S(1)}, bf16[32,3,16,128]{3,2,1,0:T(8,128)(2,1)S(1)}, u32[]{:S(2)}, u32[]{:S(2)}) %collective-permute-start.2) | collective-permute-done | bytes 393248 | tf_op jit(solution)/shard_map/ppermute | solution.py:414
  143.9 23.3 %collective-permute-done.1.refs_1_ = bf16[32,3,96,128]{3,2,1,0:T(8,128)(2,1)S(1)} collective-permute-done((bf16[32,3,96,128]{3,2,1,0:T(8,128)(2,1)S(1)}, bf16[32,3,96,128]{3,2,1,0:T(8,128)(2,1)S(1)}, u32[]{:S(2)}, u32[]{:S(2)}) %collective-permute-start.1) | collective-permute-done | bytes 2359328 | tf_op jit(solution)/shard_map/ppermute | solution.py:27
  167.3 0.8 merge.3
  168.1 1.5 copy-done
  169.6 9.5 %all-to-all-start.1 = ((bf16[32,3,112,128]{3,2,1,0:T(8,128)(2,1)}), bf16[32,3,112,128]{3,2,1,0:T(8,128)(2,1)S(1)}, u32[]{:S(2)}, u32[]{:S(2)}) async-start(bf16[32,3,112,128]{3,2,1,0:T(8,128)(2,1)} %copy-done), calls=%async_computation.1 | async-start | bytes 5505024 | tf_op jit(solution)/shard_map/all_to_all | solution.py:370
  179.1 4.0 %collective-permute-start.4 = (bf16[32,3,96,128]{3,2,1,0:T(8,128)(2,1)}, bf16[32,3,96,128]{3,2,1,0:T(8,128)(2,1)}, u32[]{:S(2)}, u32[]{:S(2)}) collective-permute-start(bf16[32,3,96,128]{3,2,1,0:T(8,128)(2,1)} %all-to-all-done.2.refs_4_), channel_id=1, source_target_pairs={{0,32},{32,64},{64,96},{160,128},{192,160},{224,192},{1,33},{33,65... | collective-permute-start | bytes 7077896 | tf_op jit(solution)/shard_map/ppermute | solution.py:417
  183.1 25.9 %collective-permute-done.4.refs_5_ = bf16[32,3,96,128]{3,2,1,0:T(8,128)(2,1)} collective-permute-done((bf16[32,3,96,128]{3,2,1,0:T(8,128)(2,1)}, bf16[32,3,96,128]{3,2,1,0:T(8,128)(2,1)}, u32[]{:S(2)}, u32[]{:S(2)}) %collective-permute-start.4) | collective-permute-done | bytes 2359328 | tf_op jit(solution)/shard_map/ppermute | solution.py:417
  209.0 10.7 %forward_kernel.1 = bf16[32,1,128,128]{3,2,1,0:T(8,128)(2,1)} custom-call(s32[1]{0:T(128)} %bitcast.stage.refs_0_, s32[64,8]{1,0:T(8,128)} %copy-done.3, f32[64,512]{1,0:T(8,128)} %copy-done.2, bf16[32,4,128,128]{3,2,1,0:T(8,128)(2,1)} %all-to-all-done.refs_3_, bf16[32,3,96,128]{3,2,1,0:T(8,128)(2,1)} %all-to-all-done.2.refs_4_, ...), custom_call_target="tpu_custom_call" | custom-call | flops 4294967296 | bytes 8388608 | tf_op jit(solution)/shard_map/forward_kernel/pallas_call | solution.py:352
  219.7 4.4 %collective-permute-start.5 = (bf16[32,1,128,128]{3,2,1,0:T(8,128)(2,1)}, bf16[32,1,128,128]{3,2,1,0:T(8,128)(2,1)}, u32[]{:S(2)}, u32[]{:S(2)}) collective-permute-start(bf16[32,1,128,128]{3,2,1,0:T(8,128)(2,1)} %forward_kernel.1), channel_id=1, source_target_pairs={{0,32},{32,64},{64,96},{96,128},{128,160},{160,192},{192,224},{1,3... | collective-permute-start | bytes 3145736 | tf_op jit(solution)/shard_map/ppermute | solution.py:27
  224.1 18.5 %all-to-all-done.1.own = bf16[32,3,112,128]{3,2,1,0:T(8,128)(2,1)S(1)} async-done(((bf16[32,3,112,128]{3,2,1,0:T(8,128)(2,1)}), bf16[32,3,112,128]{3,2,1,0:T(8,128)(2,1)S(1)}, u32[]{:S(2)}, u32[]{:S(2)}) %all-to-all-start.1) | async-done | bytes 2752544 | tf_op jit(solution)/shard_map/all_to_all | solution.py:370
  242.5 4.4 %collective-permute-start.3 = (bf16[32,3,112,128]{3,2,1,0:T(8,128)(2,1)S(1)}, bf16[32,3,112,128]{3,2,1,0:T(8,128)(2,1)S(1)}, u32[]{:S(2)}, u32[]{:S(2)}) collective-permute-start(bf16[32,3,112,128]{3,2,1,0:T(8,128)(2,1)S(1)} %all-to-all-done.1.own), channel_id=1, source_target_pairs={{32,0},{64,32},{96,64},{128,96},{160,128},{192,160},{224,192},{33,... | collective-permute-start | bytes 8257544 | tf_op jit(solution)/shard_map/ppermute | solution.py:27
  247.0 33.3 %all_to_all.20.mixed = bf16[32,1,128,128]{3,2,1,0:T(8,128)(2,1)S(1)} all-to-all(bf16[32,1,128,128]{3,2,1,0:T(8,128)(2,1)} %collective-permute-done.5), channel_id=1, replica_groups=mesh['pipe'=8,'seq'=8,'tp'=4] {'seq','tp'}, dimensions={0} | all-to-all | bytes 2097152 | tf_op jit(solution)/shard_map/all_to_all | solution.py:370
  280.3 3.2 %unpack.1 = (bf16[3,128,32,128]{3,2,1,0:T(8,128)(2,1)}, bf16[1,128,32,128]{3,2,1,0:T(8,128)(2,1)}) custom-call(s32[2]{0:T(128)S(1)} %pad_add_fusion.1.refs_0_.stage, bf16[32,3,112,128]{3,2,1,0:T(8,128)(2,1)S(1)} %all-to-all-done.1.own, bf16[32,3,112,128]{3,2,1,0:T(8,128)(2,1)S(1)} %collective-permute-done.3.late, bf16[32,1,128,128]{3,2,1,0:T(8,128)(2,1)S(1)} %all_to_all.20.mixed), custom_call_target="tpu_custom_call" | custom-call | bytes 8388608 | tf_op jit(solution)/shard_map/unpack/pallas_call | solution.py:205
  (27 shorter events, 0.5 us)
Async XLA Ops:
  4.2 104.5 %all-to-all-start = ((bf16[32,4,128,128]{3,2,1,0:T(8,128)(2,1)}), bf16[32,4,128,128]{3,2,1,0:T(8,128)(2,1)}, u32[]{:S(2)}, u32[]{:S(2)}) async-start(bf16[32,4,128,128]{3,2,1,0:T(8,128)(2,1)} %pack_first.1), calls=%async_computation | async-start | bytes 8388608 | tf_op jit(solution)/shard_map/all_to_all | solution.py:370
  16.4 10.2 %copy-start.4 = (s32[1,1,64,3]{2,1,3,0:T(1,128)S(1)}, s32[1,1,64,3]{2,1,3,0:T(1,128)}, u32[]{:S(2)}) copy-start(s32[1,1,64,3]{2,1,3,0:T(1,128)} %param.21) | copy-start | bytes 2308
  16.4 10.2 %copy-start.5 = (s32[1,1,2]{2,1,0:T(1,128)S(1)}, s32[1,1,2]{2,1,0:T(1,128)}, u32[]{:S(2)}) copy-start(s32[1,1,2]{2,1,0:T(1,128)} %param.18) | copy-start | bytes 28
  21.5 31.1 %collective-permute-start = (bf16[32,3,96,128]{3,2,1,0:T(8,128)(2,1)}, bf16[32,3,96,128]{3,2,1,0:T(8,128)(2,1)S(1)}, u32[]{:S(2)}, u32[]{:S(2)}) collective-permute-start(bf16[32,3,96,128]{3,2,1,0:T(8,128)(2,1)} %get-tuple-element.12), channel_id=1, source_target_pairs={{32,0},{64,32},{96,64},{128,160},{160,192},{192,224},{33,1},{65,33... | collective-permute-start | bytes 7077896 | tf_op jit(solution)/shard_map/ppermute | solution.py:402
  27.5 89.1 %copy-start.2 = (f32[64,512]{1,0:T(8,128)}, f32[64,512]{1,0:T(8,128)S(1)}, u32[]{:S(2)}) copy-start(f32[64,512]{1,0:T(8,128)S(1)} %select_n.9.refs_2_) | copy-start | bytes 393220
  52.6 1.7 copy-start.1
  108.7 61.0 %all-to-all-start.2 = ((bf16[32,3,96,128]{3,2,1,0:T(8,128)(2,1)}), bf16[32,3,96,128]{3,2,1,0:T(8,128)(2,1)}, u32[]{:S(2)}, u32[]{:S(2)}) async-start(bf16[32,3,96,128]{3,2,1,0:T(8,128)(2,1)} %merge.2), calls=%async_computation.2 | async-start | bytes 4718592 | tf_op jit(solution)/shard_map/all_to_all | solution.py:370
  116.6 18.7 %copy-start.3 = (s32[64,8]{1,0:T(8,128)}, s32[64,8]{1,0:T(8,128)S(1)}, u32[]{:S(2)}) copy-start(s32[64,8]{1,0:T(8,128)S(1)} %copy.23.refs_1_) | copy-start | bytes 6148
  135.3 32.0 %collective-permute-start.1 = (bf16[32,3,96,128]{3,2,1,0:T(8,128)(2,1)S(1)}, bf16[32,3,96,128]{3,2,1,0:T(8,128)(2,1)S(1)}, u32[]{:S(2)}, u32[]{:S(2)}) collective-permute-start(bf16[32,3,96,128]{3,2,1,0:T(8,128)(2,1)S(1)} %get-tuple-element.16), channel_id=1, source_target_pairs={{32,0},{64,32},{96,64},{128,96},{160,128},{192,160},{224,192},{33,... | collective-permute-start | bytes 7077896 | tf_op jit(solution)/shard_map/ppermute | solution.py:27
  139.2 4.7 %collective-permute-start.2 = (bf16[32,3,16,128]{3,2,1,0:T(8,128)(2,1)S(1)}, bf16[32,3,16,128]{3,2,1,0:T(8,128)(2,1)S(1)}, u32[]{:S(2)}, u32[]{:S(2)}) collective-permute-start(bf16[32,3,16,128]{3,2,1,0:T(8,128)(2,1)S(1)} %get-tuple-element.17), channel_id=1, source_target_pairs={{32,0},{33,1},{34,2},{35,3},{36,4},{37,5},{38,6},{39,7},{40,8},{41... | collective-permute-start | bytes 1179656 | tf_op jit(solution)/shard_map/ppermute | solution.py:414
  168.1 1.5 copy-start
  169.6 72.9 %all-to-all-start.1 = ((bf16[32,3,112,128]{3,2,1,0:T(8,128)(2,1)}), bf16[32,3,112,128]{3,2,1,0:T(8,128)(2,1)S(1)}, u32[]{:S(2)}, u32[]{:S(2)}) async-start(bf16[32,3,112,128]{3,2,1,0:T(8,128)(2,1)} %copy-done), calls=%async_computation.1 | async-start | bytes 5505024 | tf_op jit(solution)/shard_map/all_to_all | solution.py:370
  179.1 29.9 %collective-permute-start.4 = (bf16[32,3,96,128]{3,2,1,0:T(8,128)(2,1)}, bf16[32,3,96,128]{3,2,1,0:T(8,128)(2,1)}, u32[]{:S(2)}, u32[]{:S(2)}) collective-permute-start(bf16[32,3,96,128]{3,2,1,0:T(8,128)(2,1)} %all-to-all-done.2.refs_4_), channel_id=1, source_target_pairs={{0,32},{32,64},{64,96},{160,128},{192,160},{224,192},{1,33},{33,65... | collective-permute-start | bytes 7077896 | tf_op jit(solution)/shard_map/ppermute | solution.py:417
  219.7 27.3 %collective-permute-start.5 = (bf16[32,1,128,128]{3,2,1,0:T(8,128)(2,1)}, bf16[32,1,128,128]{3,2,1,0:T(8,128)(2,1)}, u32[]{:S(2)}, u32[]{:S(2)}) collective-permute-start(bf16[32,1,128,128]{3,2,1,0:T(8,128)(2,1)} %forward_kernel.1), channel_id=1, source_target_pairs={{0,32},{32,64},{64,96},{96,128},{128,160},{160,192},{192,224},{1,3... | collective-permute-start | bytes 3145736 | tf_op jit(solution)/shard_map/ppermute | solution.py:27
  242.5 37.8 %collective-permute-start.3 = (bf16[32,3,112,128]{3,2,1,0:T(8,128)(2,1)S(1)}, bf16[32,3,112,128]{3,2,1,0:T(8,128)(2,1)S(1)}, u32[]{:S(2)}, u32[]{:S(2)}) collective-permute-start(bf16[32,3,112,128]{3,2,1,0:T(8,128)(2,1)S(1)} %all-to-all-done.1.own), channel_id=1, source_target_pairs={{32,0},{64,32},{96,64},{128,96},{160,128},{192,160},{224,192},{33,... | collective-permute-start | bytes 8257544 | tf_op jit(solution)/shard_map/ppermute | solution.py:27
